TPU v7x, 32 devices: a whole 2x2x4 slice. The times are simulated.
32 devices in a mesh: section: 8 (over z, core), tensor: 4 (over y, x).
Axes of the slice: x: 2, y: 2, z: 4, core: 2. Of those that a mesh axis runs over, the one named last changes fastest.
Arguments:
- activations: bfloat16 [8, 512, 4096], P('section', None, 'tensor'), may hold values from -48 to 48
- gain: bfloat16 [8, 4096], P('section', 'tensor'), may hold values from 0.5 to 1.5
- w_query: bfloat16 [8, 4096, 4096], P('section', None, 'tensor'), may hold values from -0.0625 to 0.0625
- w_kv: bfloat16 [8, 1024, 4096], P('section', 'tensor'), may hold values from -1.8782524 to 1.8782524
- segments: int32 [8, 512], replicated, may hold values from 0 to 31, never falling along the last dimension, each value on 1 to 128 neighbouring positions
- pool: bfloat16 [16, 128, 4096], P('section', None, 'tensor'), may hold values from -48 to 48
- row_ids: int32 [32], replicated, may hold values from 0 to 15, as said below
- row_lengths: int32 [32], replicated, may hold values from 1 to 128, 512 in all
Outputs:
- after_first: bfloat16 [8, 512, 4096], P('section', None, 'tensor')
- after_second: bfloat16 [8, 512, 4096], P('section', None, 'tensor')
Inputs may be any that keep to these rules, and one draw needn't show every extreme that they name: `row_ids`: every block of 2 consecutive ids, the rows of one buffer host, is named at least once; ids may repeat.
All inputs are finite; a program needn't handle non-finite values.
Results may differ from a plain program's by a relative error of at most 0.01.
Values may be sent and summed in bfloat16 or wider, within the bound.
A program may use at most 64 MiB of HBM per device.

v0:
```python
import functools

import jax
import jax.numpy as jnp
from jax import lax
from jax.experimental import pallas as pl
from jax.experimental.pallas import tpu as pltpu
from jax.sharding import PartitionSpec as P

D = 4096
HEADS = 32
KV_HEADS = 4
HEAD_DIM = 128


norm_eps = 1e-05
masked_score = -1e30


def partner_2(block, axis, distance):
    count = lax.axis_size(axis)
    route = []
    for low in range(count):
        high = low | 1 << distance
        if high != low and high < count:
            route += [(low, high), (high, low)]
    return lax.ppermute(block, axis, route)


def from_behind(block, axis, distance):
    devices = range(lax.axis_size(axis))
    route = [(i - distance, i) for i in devices if i - distance in devices]
    return lax.ppermute(block, axis, route)


def attend(inputs, gain_cols, query_weight, keyval_weight, seg_ids, tensor_index):
    row_count, col_count = inputs.shape
    wide_inputs = inputs.astype(jnp.float32)
    square_total = lax.psum(jnp.sum(wide_inputs * wide_inputs, axis=1), "tensor")
    row_scale = lax.rsqrt(square_total / D + norm_eps)
    normed = (wide_inputs * row_scale[:, None] * gain_cols.astype(jnp.float32)[None, :]).astype(
        jnp.bfloat16
    )
    part_cols = lax.all_gather(normed, "tensor", axis=1, tiled=True)
    query_part = jnp.dot(part_cols, query_weight, preferred_element_type=jnp.float32)
    keyval_part = lax.dot_general(
        keyval_weight, part_cols, (((1,), (1,)), ((), ())), preferred_element_type=jnp.float32
    )
    query = query_part.astype(jnp.bfloat16)
    keyval = keyval_part.astype(jnp.bfloat16)
    heads_here = query_weight.shape[1] // HEAD_DIM
    group_size = HEADS // KV_HEADS
    group_devices = group_size // heads_here
    head_block = keyval
    for bit_number in range(group_devices.bit_length() - 1):
        partner = partner_2(head_block, "tensor", bit_number)
        is_lower = tensor_index // (1 << bit_number) % 2 == 0
        head_block = jnp.where(
            is_lower,
            jnp.concatenate([head_block, partner], axis=0),
            jnp.concatenate([partner, head_block], axis=0),
        )
    keys_cols = head_block[:HEAD_DIM]
    values_cols = head_block[HEAD_DIM:]
    query_heads = query.reshape(row_count, heads_here, HEAD_DIM)
    scores = jnp.einsum(
        "rhd,ds->hrs", query_heads, keys_cols, preferred_element_type=jnp.float32
    ) * HEAD_DIM ** (-0.5)
    positions = jnp.arange(row_count, dtype=jnp.int32)
    allowed = (seg_ids[:, None] == seg_ids[None, :]) & (positions[None, :] <= positions[:, None])
    scores = jnp.where(allowed[None, :, :], scores, masked_score)
    weights = jax.nn.softmax(scores, axis=-1).astype(jnp.bfloat16)
    context = jnp.einsum("hrs,ds->rhd", weights, values_cols, preferred_element_type=jnp.float32)
    context = context.astype(jnp.bfloat16).reshape(row_count, col_count)
    return (wide_inputs + context.astype(jnp.float32)).astype(jnp.bfloat16)


def pick_rows(running, host_rows, source):
    flat_rows = host_rows.reshape(-1, host_rows.shape[2])
    inside = (source >= 0) & (source < flat_rows.shape[0])
    taken = jnp.take(flat_rows, jnp.clip(source, 0, flat_rows.shape[0] - 1), axis=0)
    return jnp.where(inside[:, None], taken, running)


def per_device(activations, gain, w_query, w_kv, segments, pool, row_ids, row_lengths):
    section_index = lax.axis_index("section")
    tensor_index = lax.axis_index("tensor")
    token_count = activations.shape[1]
    col_count = activations.shape[2]
    own_segments = lax.dynamic_index_in_dim(segments, section_index, 0, keepdims=False)
    after_first = attend(activations[0], gain[0], w_query[0], w_kv[0], own_segments, tensor_index)[
        None
    ]
    ends = jnp.cumsum(row_lengths)
    positions = jnp.arange(token_count, dtype=jnp.int32)
    slot = jnp.sum((positions[:, None] >= ends[None, :]).astype(jnp.int32), axis=1)
    slot_match = slot[:, None] == jnp.arange(row_ids.shape[0], dtype=jnp.int32)[None, :]
    slot_start = jnp.sum(jnp.where(slot_match, (ends - row_lengths)[None, :], 0), axis=1)
    slot_row = jnp.sum(jnp.where(slot_match, row_ids[None, :], 0), axis=1)
    source = slot_row * pool.shape[1] + positions - slot_start
    empty_rows = jnp.zeros((token_count, col_count), jnp.bfloat16)
    fresh = pick_rows(empty_rows, lax.all_gather(pool, "section", axis=0, tiled=True), source)
    handed = from_behind(after_first, "section", 1)
    second_inputs = jnp.where(section_index == 0, fresh[None], handed)
    prior_segments = lax.dynamic_index_in_dim(
        segments, jnp.maximum(section_index - 1, 0), 0, keepdims=False
    )
    second_segments = jnp.where(section_index == 0, slot, prior_segments)
    after_second = attend(
        second_inputs[0], gain[0], w_query[0], w_kv[0], second_segments, tensor_index
    )[None]
    return (after_first, after_second)


BLOCK = 128
AT_ONCE = 4
LOG2_E = 1.4426950408889634
MESH = pl.DeviceIdType.MESH


def relay_kernel(
    sections, hosts_rows, slots,
    a_ref, gain_hbm, wq_ref, wkv_ref, seg_hbm, pool_ref, ids_hbm, len_hbm,
    out1_ref, out2_ref,
    gain_ref, seg_ref, ids_ref, len_ref, small_sem, got, weight, kv_raw, gains, normed, early, squares, query, keys, values, seg_rows, src_rows,
    pool_rows, above, below, result,
    own_send, own_recv, fwd_send, fwd_recv, gain_send, gain_recv, hand_send, hand_recv,
    x_sem, wq_sem, wkv_sem, pool_sem, mate_send, mate_recv, sum_send, sum_recv, out_sem,
):
    sec = lax.axis_index("section")
    ten = lax.axis_index("tensor")
    blocks = a_ref.shape[1] // BLOCK
    steps = 2 * blocks
    cols = a_ref.shape[2]
    over_x = ten + 1 - 2 * (ten % 2)
    over_y = ten + 2 - 4 * (ten // 2)
    peers = (ten, over_x, over_y, 3 - ten)
    even = sec % 2 == 0
    top = sections - 2

    x_copies = [
        pltpu.make_async_copy(
            a_ref.at[0, pl.ds(k * BLOCK, BLOCK)], got.at[k, 0], x_sem.at[k]
        )
        for k in range(blocks)
    ]
    wq_copies, wkv_copies = [], []
    for r in range(4):
        part = pl.ds(pl.multiple_of(peers[r] * cols, cols), cols)
        wq_copies.append(
            pltpu.make_async_copy(
                wq_ref.at[0, part], weight.at[pl.ds(r * cols, cols), pl.ds(0, cols)], wq_sem.at[r]
            )
        )
        wkv_copies.append(
            pltpu.make_async_copy(wkv_ref.at[0, :, part], kv_raw.at[r], wkv_sem.at[r])
        )
    pool_copy = pltpu.make_async_copy(pool_ref, pool_rows.at[0], pool_sem)
    small_copies = [
        pltpu.make_async_copy(src, dst, small_sem.at[i])
        for i, (src, dst) in enumerate(
            ((gain_hbm, gain_ref), (seg_hbm, seg_ref), (ids_hbm, ids_ref), (len_hbm, len_ref))
        )
    ]
    for copy in small_copies:
        copy.start()

    barrier = pltpu.get_barrier_semaphore()
    for r in (1, 2, 3):
        pl.semaphore_signal(barrier, inc=1, device_id=(sec, peers[r]), device_id_type=MESH)

    def greet(condition, other):
        @pl.when(condition)
        def _():
            pl.semaphore_signal(barrier, inc=1, device_id=(other, ten), device_id_type=MESH)

    greet(sec > 0, sec - 1)
    greet(sec < sections - 1, sec + 1)
    greet(even & (sec > 1), sec - 2)
    greet(even & (sec < top), sec + 2)
    others = 3
    for condition in (sec > 0, sec < sections - 1, even & (sec > 1), even & (sec < top)):
        others = others + jnp.where(condition, 1, 0)
    pl.semaphore_wait(barrier, others)

    def remote(src, dst, send_sem, recv_sem, device):
        return pltpu.make_async_remote_copy(
            src_ref=src, dst_ref=dst, send_sem=send_sem, recv_sem=recv_sem,
            device_id=device, device_id_type=MESH,
        )

    def own_copy(src, b, way):
        return remote(
            src, got.at[b, 1 + way], own_send.at[b, way], own_recv.at[b, way],
            (sec, peers[1 + way]),
        )

    half = BLOCK // 2

    def forward_copy(b, way):
        rows = pl.ds(way * half, half)
        return remote(
            got.at[b, 1 + way, rows], got.at[b, 3, rows], fwd_send.at[b, way],
            fwd_recv.at[b, way], (sec, peers[2 - way]),
        )

    def hand_copy(k):
        return remote(
            result.at[k], got.at[blocks + k, 0], hand_send.at[k], hand_recv.at[k], (sec + 1, ten)
        )

    def sum_copy(k):
        return remote(below.at[k], above.at[k], sum_send.at[k], sum_recv.at[k], (sec - 2, ten))

    def gain_copy(r):
        return remote(
            gains.at[0], gains.at[r], gain_send.at[r - 1], gain_recv.at[r - 1], (sec, peers[r])
        )

    mate_copy = remote(pool_ref, pool_rows.at[1], mate_send, mate_recv, (sec - 1, ten))

    for k in range(2):
        for way in range(2):
            own_copy(a_ref.at[0, pl.ds(k * BLOCK, BLOCK)], k, way).start()
    for copy in wkv_copies + x_copies[:1] + wq_copies + x_copies[1:]:
        copy.start()

    @pl.when(even)
    def _():
        pool_copy.start()

    for copy in small_copies:
        copy.wait()
    gains[0] = jnp.broadcast_to(gain_ref[...], gains.shape[1:])
    for r in (1, 2, 3):
        gain_copy(r).start()

    @pl.when(sec % 2 == 1)
    def _():
        mate_copy.start()

    positions = lax.broadcasted_iota(jnp.int32, (1, blocks * BLOCK), 1)
    start = jnp.int32(0)
    slot = jnp.zeros_like(positions)
    source = jnp.zeros_like(positions)
    for j in range(slots):
        here = positions >= start
        slot = jnp.where(here, j, slot)
        source = jnp.where(here, ids_ref[j] * pool_ref.shape[1] - start + positions, source)
        start = start + len_ref[j]
    first_segments = seg_ref[pl.ds(sec, 1), :]
    prior_segments = seg_ref[pl.ds(jnp.maximum(sec - 1, 0), 1), :]
    second_segments = jnp.where(sec == 0, slot, prior_segments)
    for k in range(blocks):
        part = slice(k * BLOCK, (k + 1) * BLOCK)
        seg_rows[k] = first_segments[:, part]
        seg_rows[blocks + k] = second_segments[:, part]
        src_rows[k] = source[:, part] - sec * hosts_rows
    keys[...] = jnp.zeros_like(keys)
    values[...] = jnp.ones_like(values)

    def picked(k):
        index = lax.broadcasted_iota(jnp.int32, (2 * hosts_rows, BLOCK), 0)
        hit = (index == src_rows[k]).astype(jnp.float32).astype(jnp.bfloat16)
        rows = pool_rows[...].reshape(2 * hosts_rows, cols)
        return lax.dot_general(
            hit, rows, (((0,), (0,)), ((), ())), preferred_element_type=jnp.float32
        )

    def pass_down(k):
        sum_copy(k).wait_recv()
        below[k] = (picked(k) + above[k].astype(jnp.float32)).astype(jnp.bfloat16)
        sum_copy(k).start()

    middle = even & (sec > 0) & (sec < top)

    for r in range(4):
        wkv_copies[r].wait()
        weight[r * cols:(r + 1) * cols, cols:] = kv_raw[r].T

    late = jnp.minimum((top - sec) // 2, 2) - 1

    for copy in wq_copies:
        copy.wait()
    for r in (1, 2, 3):
        gain_copy(r).wait_recv()

    def forward(b):
        for way in range(2):
            own_copy(got.at[b, 0], b, way).wait_recv()
            forward_copy(b, way).start()

    def scaled(b, r):
        wide = got[b, r].astype(jnp.float32)
        gain_row = gains[r].astype(jnp.float32)[0:1]
        normed[:, r * cols:(r + 1) * cols] = (wide * gain_row).astype(jnp.bfloat16)
        return jnp.sum(wide * wide, axis=1, keepdims=True)

    def begin(b):
        @pl.when(b < blocks)
        def _():
            pltpu.make_async_copy(
                a_ref.at[0, pl.ds(0, BLOCK)], got.at[b, 0], x_sem.at[b]
            ).wait()

        squares[...] = scaled(b, 0) + scaled(b, 1) + scaled(b, 2)
        for low in range(0, cols + 2 * HEAD_DIM, 256):
            early[:, low:low + 256] = jnp.dot(
                normed[:, :3 * cols], weight[:3 * cols, low:low + 256],
                preferred_element_type=jnp.float32,
            )

    forward(0)
    for way in range(2):
        own_copy(a_ref.at[0, pl.ds(2 * BLOCK, BLOCK)], 2, way).start()
    begin(0)

    def step(b, carry):
        @pl.when(b + 1 < steps)
        def _():
            forward(b + 1)

        @pl.when(even & (b == 0))
        def _():
            pool_copy.wait()
            mate_copy.wait_recv()

            @pl.when(sec == top)
            def _():
                def send(k, carry):
                    below[k] = picked(k).astype(jnp.bfloat16)
                    sum_copy(k).start()
                    return carry

                lax.fori_loop(0, blocks, send, 0)

            @pl.when(middle)
            def _():
                pass_down(0)

        down = b - late

        @pl.when(middle & (b > 0) & (down >= 1) & (down < blocks))
        def _():
            pass_down(down)

        for way in range(2):
            forward_copy(b, way).wait_recv()
        diagonal = scaled(b, 3)
        scale = lax.rsqrt((squares[...] + diagonal) / D + norm_eps)

        def project(low):
            late_part = jnp.dot(
                normed[:, 3 * cols:], weight[3 * cols:, low:low + 256],
                preferred_element_type=jnp.float32,
            )
            return ((early[:, low:low + 256] + late_part) * scale).astype(jnp.bfloat16)

        keys[0:BLOCK] = keys[BLOCK:]
        values[0:BLOCK, :HEAD_DIM] = values[BLOCK:, :HEAD_DIM]
        keyval = project(cols)
        keys[BLOCK:] = keyval[:, :HEAD_DIM]
        values[BLOCK:, :HEAD_DIM] = keyval[:, HEAD_DIM:]
        for low in range(0, cols, 256):
            two = project(low)
            query[low // HEAD_DIM] = two[:, :HEAD_DIM]
            query[low // HEAD_DIM + 1] = two[:, HEAD_DIM:]

        seg_here = seg_rows[b]
        seg_before = jnp.where(b % blocks > 0, seg_rows[jnp.maximum(b - 1, 0)], -1)
        seg_down = jnp.broadcast_to(seg_here, (BLOCK, BLOCK)).T
        row = lax.broadcasted_iota(jnp.int32, (BLOCK, BLOCK), 0)
        col = lax.broadcasted_iota(jnp.int32, (BLOCK, BLOCK), 1)
        allowed = jnp.concatenate(
            [
                jnp.where(seg_down == seg_before, 1, 0),
                jnp.where((seg_down == seg_here) & (col <= row), 1, 0),
            ],
            axis=1,
        )
        allowed = (allowed > 0)[None]
        all_keys = keys[...]
        all_values = values[...]
        for low in range(0, cols // HEAD_DIM, AT_ONCE):
            scores = lax.dot_general(
                query[low:low + AT_ONCE].reshape(AT_ONCE * BLOCK, HEAD_DIM), all_keys,
                (((1,), (1,)), ((), ())), preferred_element_type=jnp.float32,
            ).reshape(AT_ONCE, BLOCK, 2 * BLOCK) * (HEAD_DIM ** (-0.5) * LOG2_E)
            scores = jnp.where(allowed, scores, masked_score)
            powers = jnp.exp2(scores - jnp.max(scores, axis=2, keepdims=True))
            summed = jnp.dot(
                powers.astype(jnp.bfloat16).reshape(AT_ONCE * BLOCK, 2 * BLOCK), all_values,
                preferred_element_type=jnp.float32,
            ).reshape(AT_ONCE, BLOCK, 2 * HEAD_DIM)
            context = summed[:, :, :HEAD_DIM] / summed[:, :, HEAD_DIM:]
            context = context.astype(jnp.bfloat16).astype(jnp.float32)
            for h in range(AT_ONCE):
                part = slice((low + h) * HEAD_DIM, (low + h + 1) * HEAD_DIM)
                result[b, :, part] = (
                    got[b, 0, :, part].astype(jnp.float32) + context[h]
                ).astype(jnp.bfloat16)

        rows = pl.ds(pl.multiple_of((b % blocks) * BLOCK, BLOCK), BLOCK)

        @pl.when(b < blocks)
        def _():
            @pl.when(sec < sections - 1)
            def _():
                hand_copy(b).start()

            pltpu.make_async_copy(result.at[b], out1_ref.at[0, rows], out_sem.at[b]).start()

        @pl.when(b >= blocks)
        def _():
            pltpu.make_async_copy(result.at[b], out2_ref.at[0, rows], out_sem.at[b]).start()

        ahead = b + 3

        @pl.when(ahead < blocks)
        def _():
            for way in range(2):
                own_copy(
                    a_ref.at[0, pl.ds(pl.multiple_of(ahead * BLOCK, BLOCK), BLOCK)], ahead, way
                ).start()

        @pl.when((ahead >= blocks) & (ahead < steps))
        def _():
            k = ahead - blocks

            @pl.when(sec > 0)
            def _():
                hand_copy(k).wait_recv()

            @pl.when(sec == 0)
            def _():
                sum_copy(k).wait_recv()
                got[ahead, 0] = (picked(k) + above[k].astype(jnp.float32)).astype(jnp.bfloat16)

            for way in range(2):
                own_copy(got.at[ahead, 0], ahead, way).start()

        @pl.when(b + 1 < steps)
        def _():
            begin(b + 1)

        return carry

    lax.fori_loop(0, steps, step, 0)

    def drain(b, carry):
        for way in range(2):
            own_copy(got.at[b, 0], b, way).wait_send()
            forward_copy(b, way).wait_send()
        pltpu.make_async_copy(result.at[b], out1_ref.at[0, pl.ds(0, BLOCK)], out_sem.at[b]).wait()

        @pl.when(b < blocks)
        def _():
            @pl.when(sec < sections - 1)
            def _():
                hand_copy(b).wait_send()

            @pl.when(even & (sec > 0))
            def _():
                sum_copy(b).wait_send()

        return carry

    lax.fori_loop(0, steps, drain, 0)
    for r in (1, 2, 3):
        gain_copy(r).wait_send()

    @pl.when(sec % 2 == 1)
    def _():
        mate_copy.wait_send()


def relay(sections, activations, gain, w_query, w_kv, segments, pool, row_ids, row_lengths):
    tokens, cols = activations.shape[1:]
    blocks = tokens // BLOCK
    steps = 2 * blocks
    hosts_rows = pool.shape[0] * pool.shape[1]
    dma = pltpu.SemaphoreType.DMA
    bf16 = jnp.bfloat16
    anywhere = pl.BlockSpec(memory_space=pl.ANY)
    hbm = pl.BlockSpec(memory_space=pltpu.HBM)
    return pl.pallas_call(
        functools.partial(relay_kernel, sections, hosts_rows, row_ids.shape[0]),
        out_shape=(
            jax.ShapeDtypeStruct(activations.shape, bf16),
            jax.ShapeDtypeStruct(activations.shape, bf16),
        ),
        in_specs=[hbm] * 8,
        out_specs=(anywhere, anywhere),
        scratch_shapes=[
            pltpu.VMEM(gain.shape, bf16),
            pltpu.VMEM(segments.shape, jnp.int32),
            pltpu.SMEM(row_ids.shape, jnp.int32),
            pltpu.SMEM(row_lengths.shape, jnp.int32),
            dma((4,)),
            pltpu.VMEM((steps, 4, BLOCK, cols), bf16),
            pltpu.VMEM((4 * cols, cols + 2 * HEAD_DIM), bf16),
            pltpu.VMEM((4, 2 * HEAD_DIM, cols), bf16),
            pltpu.VMEM((4, 16, cols), bf16),
            pltpu.VMEM((BLOCK, 4 * cols), bf16),
            pltpu.VMEM((BLOCK, cols + 2 * HEAD_DIM), jnp.float32),
            pltpu.VMEM((BLOCK, 1), jnp.float32),
            pltpu.VMEM((cols // HEAD_DIM, BLOCK, HEAD_DIM), bf16),
            pltpu.VMEM((2 * BLOCK, HEAD_DIM), bf16),
            pltpu.VMEM((2 * BLOCK, 2 * HEAD_DIM), bf16),
            pltpu.VMEM((steps, 1, BLOCK), jnp.int32),
            pltpu.VMEM((blocks, 1, BLOCK), jnp.int32),
            pltpu.VMEM((2, *pool.shape), bf16),
            pltpu.VMEM((blocks, BLOCK, cols), bf16),
            pltpu.VMEM((blocks, BLOCK, cols), bf16),
            pltpu.VMEM((steps, BLOCK, cols), bf16),
            dma((steps, 2)), dma((steps, 2)), dma((steps, 2)), dma((steps, 2)),
            dma((3,)), dma((3,)), dma((blocks,)), dma((blocks,)),
            dma((blocks,)), dma((4,)), dma((4,)), dma, dma, dma,
            dma((blocks,)), dma((blocks,)), dma((steps,)),
        ],
        compiler_params=pltpu.CompilerParams(
            collective_id=0, has_side_effects=True, vmem_limit_bytes=48 * 1024 * 1024
        ),
    )(
        *(
            pltpu.with_memory_space_constraint(argument, pltpu.HBM)
            for argument in (
                activations, gain, w_query, w_kv, segments, pool, row_ids, row_lengths
            )
        )
    )


def solution(mesh):
    square = (
        mesh.shape["tensor"] == KV_HEADS == 4
        and mesh.shape["section"] % 2 == 0
        and mesh.shape["section"] >= 4
    )
    body = functools.partial(relay, mesh.shape["section"]) if square else per_device
    return jax.shard_map(
        body,
        mesh=mesh,
        in_specs=(
            P("section", None, "tensor"),
            P("section", "tensor"),
            P("section", None, "tensor"),
            P("section", "tensor", None),
            P(),
            P("section", None, "tensor"),
            P(),
            P(),
        ),
        out_specs=(P("section", None, "tensor"), P("section", None, "tensor")),
        check_vma=False,
    )
```

profile of v0, /device:TPU:0, one launch (start us, length us, event | category | flops | bytes accessed | tf_op | source)
XLA Modules:
  0.0 82.3 jit_solution(11802079433866658848)
XLA Ops:
  0.6 79.8 %shard_map.95 = (bf16[1,512,1024]{2,1,0:T(8,128)(2,1)S(1)}, bf16[1,512,1024]{2,1,0:T(8,128)(2,1)S(1)}) custom-call(bf16[1,512,1024]{2,1,0:T(8,128)(2,1)} %a_ref.1, bf16[1,1024]{1,0:T(2,128)(2,1)} %gain_hbm.1, bf16[1,4096,1024]{2,1,0:T(8,128)(2,1)} %wq_ref.1, bf16[1,256,4096]{2,1,0:T(8,128)(2,1)} %wkv_ref.1, s32[8,512]{1,0:T(8,128)} %seg_hbm.1, ...), custom_call_target="tpu_custom_call" | custom-call | tf_op jit(solution)/shard_map/pallas_call | solution.py:486
  80.4 1.0 %copy.12 = bf16[1,512,1024]{2,1,0:T(8,128)(2,1)} copy(bf16[1,512,1024]{2,1,0:T(8,128)(2,1)S(1)} %get-tuple-element.4) | data formatting | bytes 2097152
  81.4 1.0 %copy.13 = bf16[1,512,1024]{2,1,0:T(8,128)(2,1)} copy(bf16[1,512,1024]{2,1,0:T(8,128)(2,1)S(1)} %get-tuple-element.5) | data formatting | bytes 2097152
where the time goes:
time: 82.5 us; the launch traced here: 82.3 us
  Pallas kernels  79.8 us (97%)
  local copies, waits for them, and re-layouts  1.94 us (2%)
    pallas_call x1, Pallas kernels, relay(): pl.pallas_call(functools.partial(relay_kernel, sections, hosts_rows, row_...  79.8 us
    unnamed x2, local copies, waits for them, and re-layouts  1.94 us

commit v1 on v0

--- a/solution.py
+++ b/solution.py
@@ -311,8 +311,12 @@
             )
 
     forward(0)
-    for way in range(2):
-        own_copy(a_ref.at[0, pl.ds(2 * BLOCK, BLOCK)], 2, way).start()
+
+    @pl.when(even)
+    def _():
+        for way in range(2):
+            own_copy(a_ref.at[0, pl.ds(2 * BLOCK, BLOCK)], 2, way).start()
+
     begin(0)
 
     def step(b, carry):
@@ -414,7 +418,7 @@
         def _():
             pltpu.make_async_copy(result.at[b], out2_ref.at[0, rows], out_sem.at[b]).start()
 
-        ahead = b + 3
+        ahead = b + 3 - sec % 2
 
         @pl.when(ahead < blocks)
         def _():

time: 82.5 us -> 85.5 us (1.036)
  the two profiles are of different devices: /device:TPU:0 before, /device:TPU:1 now
where the time goes in v1:
time: 85.5 us; the launch traced here: 85.3 us
  Pallas kernels  82.7 us (97%)
  local copies, waits for them, and re-layouts  1.94 us (2%)
    pallas_call x1, Pallas kernels, relay(): pl.pallas_call(functools.partial(relay_kernel, sections, hosts_rows, row_...  82.7 us
    unnamed x2, local copies, waits for them, and re-layouts  1.94 us

profile of v1, /device:TPU:1, one launch (start us, length us, event | category | flops | bytes accessed | tf_op | source)
XLA Modules:
  0.0 85.3 jit_solution(3885297081266363701)
XLA Ops:
  0.6 82.7 %shard_map.95 = (bf16[1,512,1024]{2,1,0:T(8,128)(2,1)S(1)}, bf16[1,512,1024]{2,1,0:T(8,128)(2,1)S(1)}) custom-call(bf16[1,512,1024]{2,1,0:T(8,128)(2,1)} %a_ref.1, bf16[1,1024]{1,0:T(2,128)(2,1)} %gain_hbm.1, bf16[1,4096,1024]{2,1,0:T(8,128)(2,1)} %wq_ref.1, bf16[1,256,4096]{2,1,0:T(8,128)(2,1)} %wkv_ref.1, s32[8,512]{1,0:T(8,128)} %seg_hbm.1, ...), custom_call_target="tpu_custom_call" | custom-call | tf_op jit(solution)/shard_map/pallas_call | solution.py:490
  83.4 1.0 %copy.12 = bf16[1,512,1024]{2,1,0:T(8,128)(2,1)} copy(bf16[1,512,1024]{2,1,0:T(8,128)(2,1)S(1)} %get-tuple-element.4) | data formatting | bytes 2097152
  84.3 1.0 %copy.13 = bf16[1,512,1024]{2,1,0:T(8,128)(2,1)} copy(bf16[1,512,1024]{2,1,0:T(8,128)(2,1)S(1)} %get-tuple-element.5) | data formatting | bytes 2097152
